TPU v7x, 32 devices: a whole 2x2x4 slice. The times are simulated.
32 devices in a mesh: dp: 8 (over z, y), head: 4 (over x, core).
Axes of the slice: x: 2, y: 2, z: 4, core: 2. Of those that a mesh axis runs over, the one named last changes fastest.
Arguments:
- hidden_in: bfloat16 [2048, 2048], P(('dp', 'head')), may hold values from -6 to 6
- norm_gain: bfloat16 [2048], replicated, may hold values from 0.25 to 1.75
- w_query: bfloat16 [2048, 2048], P(None, 'head'), may hold values from -0.125 to 0.125
- key_weight: bfloat16 [2048, 1024], P(None, 'head'), may hold values from -0.125 to 0.125
- w_value: bfloat16 [2048, 1024], P(None, 'head'), may hold values from -0.125 to 0.125
- query_gain: bfloat16 [128], replicated, may hold values from 0.796875 to 4
- key_gain: bfloat16 [128], replicated, may hold values from 0.25 to 1.75
- w_out: bfloat16 [2048, 2048], P('head'), may hold values from -0.125 to 0.125
- prefix_root_keys: bfloat16 [1024, 1024], P('dp', 'head'), may hold values from -210 to 210
- prefix_root_values: bfloat16 [1024, 1024], P('dp', 'head'), may hold values from -6 to 6
- mid_keys: bfloat16 [4096, 1024], P('dp', 'head'), may hold values from -210 to 210
- mid_values: bfloat16 [4096, 1024], P('dp', 'head'), may hold values from -6 to 6
- mid_lengths: int32 [16], replicated, may hold values from 1 to 256, 2048 in all
- leaf_keys: bfloat16 [4096, 1024], P('dp', 'head'), may hold values from -6 to 6
- leaf_values: bfloat16 [4096, 1024], P('dp', 'head'), may hold values from -6 to 6
- leaf_lengths: int32 [64], P('dp'), may hold values from 1 to 64, 2048 in all
- token_request: int32 [8, 256], P('dp'), may hold values from 0 to 7, never falling along the last dimension, each value on 1 to 64 neighbouring positions
- request_node: int32 [8, 8], P('dp'), may hold values from 0 to 15, as said below
Outputs:
- attn_update: bfloat16 [2048, 2048], P(('dp', 'head'))
- cache_keys: bfloat16 [2048, 1024], P('dp', 'head')
- cache_values: bfloat16 [2048, 1024], P('dp', 'head')
Inputs may be any that keep to these rules, and one draw needn't show every extreme that they name: `token_request`: in each row requests 0 to 7 all occur, in rising order, each on 1 to 64 consecutive tokens; some request has exactly 64. `request_node`: node v is held by dp index v // 2; the 8 requests of one row have parents on 8 different dp indices, one each.
All inputs are finite; a program needn't handle non-finite values. No bound on the sum of `leaf_lengths` on one device may be relied on, other than what follows from the above.
Results may differ from a plain program's by a relative error of at most 0.039.
Values may be sent and summed in bfloat16 or wider, within the bound.
A program may use at most 128 MiB of HBM per device.

v0:
```python
import math
import jax
import jax.numpy as jnp
from jax import lax
from jax.sharding import PartitionSpec as P

MID_DEV = 2
MID_LEN = 256
EPS = 1e-06
THETA = 1000000.0
MASKED = -1e30


def rms_rows(values, gain):
    power = jnp.mean(values * values, axis=-1, keepdims=True)
    return values * lax.rsqrt(power + EPS) * gain


def rotate(values, positions):
    width = values.shape[-1]
    half = width // 2
    exponent = jnp.arange(half).astype(jnp.float32) * (2.0 / width)
    freqs = jnp.power(THETA, -exponent)
    angles = positions.astype(jnp.float32)[:, None] * freqs[None, :]
    cosine = jnp.cos(angles)[:, None, :]
    sine = jnp.sin(angles)[:, None, :]
    first = values[..., :half]
    second = values[..., half:]
    return jnp.concatenate(
        [first * cosine - second * sine, second * cosine + first * sine], axis=-1
    )


def attend_over_block(query_matrix, keys, values, lengths, kv_heads, head_dim):
    blocks, slots, width = query_matrix.shape
    query_group = width // (kv_heads * head_dim)
    span = keys.shape[1]
    heads_query = query_matrix.reshape(blocks, slots, kv_heads, query_group, head_dim)
    key_heads = keys.reshape(blocks, span, kv_heads, head_dim)
    value_heads = values.reshape(blocks, span, kv_heads, head_dim)
    scores = jnp.einsum(
        "bskgd,blkd->bskgl", heads_query, key_heads, preferred_element_type=jnp.float32
    ) / math.sqrt(head_dim)
    live = jnp.arange(span, dtype=jnp.int32)[None, :] < lengths[:, None]
    scores = jnp.where(live[:, None, None, None, :], scores, MASKED)
    highest = jnp.max(scores, axis=-1)
    weights = jnp.exp(scores - highest[..., None])
    total = jnp.sum(weights, axis=-1)
    summed = jnp.einsum(
        "bskgl,blkd->bskgd",
        weights.astype(jnp.bfloat16),
        value_heads,
        preferred_element_type=jnp.float32,
    )
    output = (summed / total[..., None]).astype(jnp.bfloat16).reshape(blocks, slots, width)
    log_total = (highest + jnp.log(total)).reshape(blocks, slots, kv_heads * query_group)
    return (output, log_total)


def body(
    hidden_in,
    norm_gain,
    w_query,
    key_weight,
    w_value,
    query_gain,
    key_gain,
    w_out,
    prefix_root_keys,
    prefix_root_values,
    mid_keys,
    mid_values,
    mid_lengths,
    leaf_keys,
    leaf_values,
    leaf_lengths,
    token_request,
    request_node,
):
    head_dim = query_gain.shape[0]
    query_width = w_query.shape[1]
    key_width = key_weight.shape[1]
    kv_heads = key_width // head_dim
    query_group = query_width // key_width
    scale = 1.0 / math.sqrt(head_dim)
    dp_count = lax.axis_size("dp")
    normalized_input = rms_rows(
        hidden_in.astype(jnp.float32), norm_gain.astype(jnp.float32)
    ).astype(jnp.bfloat16)
    piece = lax.all_gather(normalized_input, "head", axis=0, tiled=True)
    mixed = jnp.concatenate(
        [
            jnp.dot(piece, w_query, preferred_element_type=jnp.float32),
            jnp.dot(piece, key_weight, preferred_element_type=jnp.float32),
            jnp.dot(piece, w_value, preferred_element_type=jnp.float32),
        ],
        axis=1,
    )
    height = mixed.shape[0]
    segment = token_request[0]
    branch_nodes = request_node[0]
    requests = branch_nodes.shape[0]
    request_ids = jnp.arange(requests, dtype=jnp.int32)
    token_ids = jnp.arange(height, dtype=jnp.int32)
    member = segment[None, :] == request_ids[:, None]
    counts = jnp.sum(member.astype(jnp.int32), axis=1)
    starts = jnp.cumsum(counts) - counts
    offset = token_ids - jnp.sum(jnp.where(member, starts[:, None], 0), axis=0)
    node_total = mid_lengths.shape[0]
    node_match = branch_nodes[:, None] == jnp.arange(node_total, dtype=jnp.int32)[None, :]
    branch_length = jnp.sum(jnp.where(node_match, mid_lengths[None, :], 0), axis=1)
    root_total = prefix_root_keys.shape[0] * dp_count
    positions = (
        root_total
        + jnp.sum(jnp.where(member, (branch_length + leaf_lengths)[:, None], 0), axis=0)
        + offset
    )
    query_part = mixed[:, :query_width].reshape(height, query_width // head_dim, head_dim)
    key_portion = mixed[:, query_width : query_width + key_width].reshape(
        height, kv_heads, head_dim
    )
    query_matrix = rotate(rms_rows(query_part, query_gain.astype(jnp.float32)), positions).astype(
        jnp.bfloat16
    )
    new_keys = rotate(rms_rows(key_portion, key_gain.astype(jnp.float32)), positions).astype(
        jnp.bfloat16
    )
    new_values = mixed[:, query_width + key_width :].astype(jnp.bfloat16)
    heads_query = query_matrix.reshape(height, kv_heads, query_group, head_dim)
    query_rows = query_matrix.reshape(height, query_width)
    capacity = 2 * height // dp_count
    slot_ids = jnp.arange(capacity, dtype=jnp.int32)
    req_valid = slot_ids[None, :] < counts[:, None]
    req_picks = jnp.where(req_valid, starts[:, None] + slot_ids[None, :], 0).reshape(-1)
    req_queries = jnp.take(query_rows, req_picks, axis=0).reshape(
        requests, capacity, kv_heads, query_group, head_dim
    )
    req_keys = jnp.take(new_keys, req_picks, axis=0).reshape(requests, capacity, kv_heads, head_dim)
    req_values = jnp.take(new_values, req_picks, axis=0).reshape(
        requests, capacity, kv_heads, head_dim
    )
    leaf_each = leaf_keys.shape[0] // requests
    leaf_heads_key = leaf_keys.reshape(requests, leaf_each, kv_heads, head_dim)
    leaf_heads_value = leaf_values.reshape(requests, leaf_each, kv_heads, head_dim)
    own_live = (slot_ids[None, :] <= slot_ids[:, None])[None, :, :] & req_valid[:, None, :]
    leaf_live = jnp.arange(leaf_each, dtype=jnp.int32)[None, :] < leaf_lengths[:, None]
    own_scores = (
        jnp.einsum("rskgd,rlkd->rskgl", req_queries, req_keys, preferred_element_type=jnp.float32)
        * scale
    )
    leaf_scores = (
        jnp.einsum(
            "rskgd,rlkd->rskgl", req_queries, leaf_heads_key, preferred_element_type=jnp.float32
        )
        * scale
    )
    own_mask = own_live[:, :, None, None, :]
    leaf_mask = leaf_live[:, None, None, None, :]
    own_scores = jnp.where(own_mask, own_scores, MASKED)
    leaf_scores = jnp.where(leaf_mask, leaf_scores, MASKED)
    req_top = jnp.maximum(jnp.max(own_scores, axis=-1), jnp.max(leaf_scores, axis=-1))
    own_weights = jnp.where(own_mask, jnp.exp(own_scores - req_top[..., None]), 0.0)
    leaf_weights = jnp.where(leaf_mask, jnp.exp(leaf_scores - req_top[..., None]), 0.0)
    req_total = jnp.sum(own_weights, axis=-1) + jnp.sum(leaf_weights, axis=-1)
    req_summed = jnp.einsum(
        "rskgl,rlkd->rskgd",
        own_weights.astype(jnp.bfloat16),
        req_values,
        preferred_element_type=jnp.float32,
    )
    req_summed = req_summed + jnp.einsum(
        "rskgl,rlkd->rskgd",
        leaf_weights.astype(jnp.bfloat16),
        leaf_heads_value,
        preferred_element_type=jnp.float32,
    )
    token_slot = jnp.sum(jnp.where(member, (request_ids * capacity)[:, None], 0), axis=0) + offset
    highest = jnp.take(
        req_top.reshape(requests * capacity, kv_heads, query_group), token_slot, axis=0
    )
    total = jnp.take(
        req_total.reshape(requests * capacity, kv_heads, query_group), token_slot, axis=0
    )
    summed = jnp.take(
        req_summed.reshape(requests * capacity, kv_heads, query_group, head_dim), token_slot, axis=0
    )
    piece = (
        lax.all_gather(prefix_root_keys, "dp", axis=0, tiled=True),
        lax.all_gather(prefix_root_values, "dp", axis=0, tiled=True),
    )
    running = total
    gathered = summed
    key_piece = piece[0].reshape(-1, kv_heads, head_dim)
    value_piece = piece[1].reshape(-1, kv_heads, head_dim)
    scores = (
        jnp.einsum("tkgd,skd->tkgs", heads_query, key_piece, preferred_element_type=jnp.float32)
        * scale
    )
    new_top = jnp.maximum(highest, jnp.max(scores, axis=-1))
    shrink = jnp.exp(highest - new_top)
    weights = jnp.exp(scores - new_top[..., None])
    running = running * shrink + jnp.sum(weights, axis=-1)
    gathered = gathered * shrink[..., None] + jnp.einsum(
        "tkgs,skd->tkgd",
        weights.astype(jnp.bfloat16),
        value_piece,
        preferred_element_type=jnp.float32,
    )
    owner_of = branch_nodes // MID_DEV
    owner_ids = jnp.arange(dp_count, dtype=jnp.int32)
    owner_match = owner_of[None, :] == owner_ids[:, None]
    block_start = jnp.sum(jnp.where(owner_match, starts[None, :], 0), axis=1)
    block_count = jnp.sum(jnp.where(owner_match, counts[None, :], 0), axis=1)
    block_slot = jnp.sum(jnp.where(owner_match, (branch_nodes % MID_DEV)[None, :], 0), axis=1)
    block_length = jnp.sum(jnp.where(owner_match, branch_length[None, :], 0), axis=1)
    valid = slot_ids[None, :] < block_count[:, None]
    picks = jnp.where(valid, block_start[:, None] + slot_ids[None, :], 0).reshape(-1)
    query_buffer = jnp.take(query_rows, picks, axis=0).reshape(dp_count, capacity, query_width)
    query_buffer = jnp.where(valid[..., None], query_buffer, jnp.zeros((), jnp.bfloat16))
    wanted = lax.all_to_all(block_slot[:, None], "dp", split_axis=0, concat_axis=0, tiled=True)[
        :, 0
    ]
    own_keys = mid_keys.reshape(MID_DEV, MID_LEN, key_width)
    own_values = mid_values.reshape(MID_DEV, MID_LEN, key_width)
    sent_keys = jnp.take(own_keys, wanted, axis=0)
    sent_values = jnp.take(own_values, wanted, axis=0)
    got_keys, got_values = (
        lax.all_to_all(sent_keys, "dp", split_axis=0, concat_axis=0, tiled=True),
        lax.all_to_all(sent_values, "dp", split_axis=0, concat_axis=0, tiled=True),
    )
    middle_output, middle_log_sum = attend_over_block(
        query_buffer, got_keys, got_values, block_length, kv_heads, head_dim
    )
    flattened_rows = jnp.sum(jnp.where(member, (owner_of * capacity)[:, None], 0), axis=0) + offset
    middle_rows = (
        jnp.take(middle_output.reshape(dp_count * capacity, query_width), flattened_rows, axis=0)
        .astype(jnp.float32)
        .reshape(height, kv_heads, query_group, head_dim)
    )
    middle_maximum = jnp.take(
        middle_log_sum.reshape(dp_count * capacity, kv_heads * query_group), flattened_rows, axis=0
    ).reshape(height, kv_heads, query_group)
    joint = jnp.maximum(new_top, middle_maximum)
    near_part = jnp.exp(new_top - joint)
    far_part = jnp.exp(middle_maximum - joint)
    attn = (near_part[..., None] * gathered + far_part[..., None] * middle_rows) / (
        near_part * running + far_part
    )[..., None]
    attn = attn.reshape(height, query_width).astype(jnp.bfloat16)
    update = lax.psum_scatter(
        jnp.dot(attn, w_out, preferred_element_type=jnp.float32).astype(jnp.bfloat16),
        "head",
        scatter_dimension=0,
        tiled=True,
    )
    return (update, new_keys.reshape(height, key_width), new_values)


def solution(mesh):
    in_specs = (
        P(("dp", "head"), None),
        P(),
        P(None, "head"),
        P(None, "head"),
        P(None, "head"),
        P(),
        P(),
        P("head", None),
        P("dp", "head"),
        P("dp", "head"),
        P("dp", "head"),
        P("dp", "head"),
        P(),
        P("dp", "head"),
        P("dp", "head"),
        P("dp"),
        P("dp", None),
        P("dp", None),
    )
    out_specs = (P(("dp", "head"), None), P("dp", "head"), P("dp", "head"))
    return jax.shard_map(body, mesh=mesh, in_specs=in_specs, out_specs=out_specs, check_vma=False)
```

profile of v0, /device:TPU:0, one launch (start us, length us, event | category | flops | bytes accessed | tf_op | source)
XLA Modules:
  0.0 225.4 jit_solution(1173646855730605797)
XLA Ops:
  7.2 0.9 convert_reduce_fusion
  9.7 0.9 select_reduce_fusion.8
  11.3 7.3 %all-to-all-start = ((s32[8,1,1]{2,1,0:T(1,128)}), s32[8,1,1]{2,1,0:T(1,128)S(1)}, u32[]{:S(2)}, u32[]{:S(2)}) async-start(s32[8,1,1]{2,1,0:T(1,128)} %copy.295), calls=%async_computation | async-start | bytes 8192 | tf_op jit(solution)/shard_map/all_to_all | solution.py:220
  18.7 1.1 fusion.44
  19.8 0.7 convert_element_type.80
  20.5 1.8 fusion.46
  22.3 0.7 add.259
  23.0 1.3 iota_compare_fusion.5
  26.5 1.2 convert_element_type.86
  27.8 1.2 convert_element_type.82
  29.6 0.8 select_reduce_fusion
  32.8 0.9 copy.293
  33.8 1.7 reshape.513
  35.5 0.8 reshape.518
  36.3 29.8 %all_gather.10 = bf16[1024,256]{0,1:T(8,128)(2,1)} all-gather(bf16[128,256]{0,1:T(8,128)(2,1)S(1)} %copy.293), channel_id=1, replica_groups=mesh['dp'=8,'head'=4] {'dp'}, dimensions={0}, use_global_device_ids=true | all-gather | bytes 589824 | tf_op jit(solution)/shard_map/all_gather | solution.py:188
  66.0 0.8 broadcast_and_fusion
  67.5 31.3 %all_gather.11 = bf16[1024,256]{1,0:T(8,128)(2,1)S(1)} all-gather(bf16[128,256]{1,0:T(8,128)(2,1)S(1)} %copy-done.17), channel_id=1, replica_groups=mesh['dp'=8,'head'=4] {'dp'}, dimensions={0}, use_global_device_ids=true | all-gather | bytes 589824 | tf_op jit(solution)/shard_map/all_gather | solution.py:189
  98.7 1.2 multiply_cosine_fusion
  99.9 1.1 copy.311
  102.4 2.6 %gather_fusion.7 = bf16[8,256,256]{2,1,0:T(8,128)(2,1)} fusion(bf16[2,256,256]{2,1,0:T(8,128)(2,1)} %bitcast.146, s32[1024]{0:T(1024)S(1)} %pad_clamp_fusion.3), kind=kCustom, calls=%fused_computation.2.clone | custom fusion | bytes 2097184 | tf_op jit(solution)/shard_map/jit(_take)/gather | solution.py:225
  105.0 2.8 %broadcast_select_fusion = (bf16[8,256,256]{2,1,0:T(8,128)(2,1)}, bf16[8,256,256]{2,1,0:T(8,128)(2,1)}) fusion(bf16[8,256,256]{2,1,0:T(8,128)(2,1)S(1)} %gather_fusion.9, pred[8]{0:T(512)(128)(4,1)S(1)} %compare_and_fusion.2, bf16[8,256,256]{2,1,0:T(8,128)(2,1)} %gather_fusion.7), kind=kLoop, calls=%fused_computation.48 | loop fusion | flops 1048576 | bytes 4194312 | tf_op jit(solution)/shard_map/jit(_take)/select_n | solution.py:226
  107.9 4.4 %all-to-all-start.1 = ((bf16[8,256,256]{2,1,0:T(8,128)(2,1)}), bf16[8,256,256]{2,1,0:T(8,128)(2,1)}, u32[]{:S(2)}, u32[]{:S(2)}) async-start(bf16[8,256,256]{2,1,0:T(8,128)(2,1)} %get-tuple-element.34), calls=%async_computation.1 | async-start | bytes 2097152 | tf_op jit(solution)/shard_map/all_to_all | solution.py:228
  112.3 2.6 %fusion.89 = f32[256,512]{1,0:T(8,128)S(1)} fusion(bf16[256,2048]{1,0:T(8,128)(2,1)} %all-gather.2.cloned.1.call-done, bf16[2048,512]{1,0:T(8,128)(2,1)} %param.26), kind=kOutput, calls=%fused_computation.188 | convolution fusion | flops 536870912 | bytes 3670016 | tf_op jit(solution)/shard_map/dot_general | solution.py:93
  116.5 0.7 copy.291
  117.2 1.0 pad_maximum_fusion
  118.2 0.7 copy.292
  119.5 2.6 %gather_fusion.2 = bf16[512,256]{1,0:T(8,128)(2,1)} fusion(bf16[256,256]{1,0:T(8,128)(2,1)S(1)} %convolution_convert_fusion.1, s32[1024]{0:T(1024)S(1)} %pad_clamp_fusion.6), kind=kCustom, calls=%fused_computation.8 | custom fusion | bytes 526336 | tf_op jit(solution)/shard_map/jit(_take)/gather | solution.py:139
  122.0 1.7 gather.42
  123.8 2.5 %multiply_reduce_fusion.1 = (f32[256,2]{0,1:T(2,128)S(1)}, f32[256,256]{0,1:T(8,128)}) fusion(bf16[256,2048]{1,0:T(8,128)(2,1)S(1)} %copy-done.5, bf16[2048,256]{1,0:T(8,128)(2,1)} %param.27), kind=kOutput, calls=%fused_computation.97 | convolution fusion | flops 268566016 | bytes 2361344 | tf_op jit(solution)/shard_map/dot_general | solution.py:94
  126.2 1.1 copy.280
  128.7 2.1 gather_fusion
  130.9 2.0 gather_fusion.8
  132.9 0.9 broadcast_select_fusion.2
  133.9 2.0 reshape.517
  135.9 2.0 gather_fusion.5
  137.9 0.9 broadcast_select_fusion.3
  138.8 1.2 reshape.512
  140.2 2.6 %fusion.88 = (f32[8,64,2,2]{1,3,2,0:T(2,128)S(1)}, f32[8,64,2,2,64]{1,4,3,2,0:T(8,128)}) fusion(bf16[8,64,2,128,1]{3,2,1,0,4:T(2,128)(2,1)} %bitcast.161, bf16[8,64,2,2,128]{4,3,2,1,0:T(2,128)(2,1)S(1)} %reshape.512, pred[8,64]{1,0:T(8,128)(4,1)S(1)} %copy-done.21), kind=kOutput, calls=%fused_computation.187 | convolution fusion | flops 33945600 | bytes 1319424 | tf_op jit(solution)/shard_map/rskgd,rlkd->rskgl/dot_general | solution.py:152
  142.8 1.7 fusion.87
  144.6 1.1 copy.332
  145.6 1.3 convolution_bitcast_fusion.2
  147.6 1.8 copy.309
  149.4 3.4 %gather_fusion.3 = f32[256,2,2,128]{3,2,1,0:T(2,128)} fusion(f32[512,2,2,128]{3,2,1,0:T(2,128)} %copy.309, s32[1024]{0:T(1024)} %pad_clamp_fusion), kind=kCustom, calls=%fused_computation.9 | custom fusion | bytes 1049600 | tf_op jit(solution)/shard_map/jit(_take)/gather | solution.py:184
  152.8 2.0 copy.310
  154.8 5.7 %all-to-all-start.2 = ((bf16[8,256,256]{2,1,0:T(8,128)(2,1)}), bf16[8,256,256]{2,1,0:T(8,128)(2,1)}, u32[]{:S(2)}, u32[]{:S(2)}) async-start(bf16[8,256,256]{2,1,0:T(8,128)(2,1)} %get-tuple-element.33), calls=%async_computation.2 | async-start | bytes 2097152 | tf_op jit(solution)/shard_map/all_to_all | solution.py:229
  160.8 1.8 fusion.42
  162.9 1.8 gather_fusion.10
  164.7 1.1 copy.317
  165.8 2.2 gather_fusion.6
  168.1 1.8 bitcast_reduce_fusion
  169.9 1.9 copy-done.2
  171.8 0.9 fusion.1
  172.8 1.5 copy.296
  174.3 1.7 bitcast_reduce_fusion.1
  175.9 1.3 copy-done.7
  177.3 0.9 fusion.9
  178.2 1.5 copy.312
  179.7 3.2 %fusion.16 = bf16[8,64,2,2,128]{4,1,3,2,0:T(8,128)(2,1)} fusion(bf16[8,256,2,128,1]{1,3,4,2,0:T(8,128)(2,1)S(1)} %bitcast.158, f32[8,2,256,64,2]{2,3,4,1,0:T(8,128)} %copy-done.7, f32[8,64,2,2]{1,3,2,0:T(2,128)S(1)} %get-tuple-element.47, pred[8,256]{1,0:T(8,128)(4,1)S(1)} %copy-done.19, f32[8,64,2,2]{1,3,2,0:T(2,128)S(1)} %fusion.9), kind=kOutput, calls=%fused_computation.37 | convolution fusion | flops 136839168 | bytes 3688448 | tf_op jit(solution)/shard_map/bskgl,blkd->bskgd/dot_general | solution.py:49
  183.0 1.6 copy.314
  184.8 1.2 gather_fusion.4
  186.2 0.7 gather_fusion.1
  187.1 3.5 %fusion.37 = bf16[256,2,2,128]{0,3,2,1:T(8,128)(2,1)S(1)} fusion(bf16[1024,2,128,1]{0,2,3,1:T(8,128)(2,1)} %bitcast.160, f32[2,256,2,1024]{3,1,2,0:T(8,128)} %copy-done.2, f32[256,2,2]{0,2,1:T(2,128)S(1)} %fusion.74, f32[256,2,2,128]{0,3,2,1:T(8,128)} %copy.310, f32[256,2,2]{0,2,1:T(2,128)S(1)} %get-tuple-element.16, ...), kind=kOutput, calls=%fused_computation.52 | convolution fusion | flops 272891904 | bytes 5788160 | tf_op jit(solution)/shard_map/tkgs,skd->tkgd/dot_general | solution.py:203
  190.7 1.7 convolution_convert_fusion
  193.1 25.5 %reduce-scatter.2.cloned.1.call-done = bf16[64,2048]{1,0:T(8,128)(2,1)} async-done(((bf16[256,2048]{1,0:T(8,128)(2,1)}), bf16[64,2048]{1,0:T(8,128)(2,1)}) %reduce-scatter.2.cloned.1.call-update) | async-done | bytes 262160 | tf_op jit(solution)/shard_map/reduce_scatter | solution.py:250
  (136 shorter events, 16.0 us)
Async XLA Ops:
  7.2 183.5 %copy-start = (bf16[512,2048]{1,0:T(8,128)(2,1)S(1)}, bf16[512,2048]{1,0:T(8,128)(2,1)}, u32[]{:S(2)}) copy-start(bf16[512,2048]{1,0:T(8,128)(2,1)} %param.31) | copy-start | bytes 6291460
  7.2 28.3 %copy-start.16 = (bf16[512,256]{1,0:T(8,128)(2,1)S(1)}, bf16[512,256]{1,0:T(8,128)(2,1)}, u32[]{:S(2)}) copy-start(bf16[512,256]{1,0:T(8,128)(2,1)} %param.38) | copy-start | bytes 786436
  7.2 60.3 %copy-start.17 = (bf16[128,256]{1,0:T(8,128)(2,1)S(1)}, bf16[128,256]{1,0:T(8,128)(2,1)}, u32[]{:S(2)}) copy-start(bf16[128,256]{1,0:T(8,128)(2,1)} %param.33) | copy-start | bytes 196612
  11.3 89.6 %all-to-all-start = ((s32[8,1,1]{2,1,0:T(1,128)}), s32[8,1,1]{2,1,0:T(1,128)S(1)}, u32[]{:S(2)}, u32[]{:S(2)}) async-start(s32[8,1,1]{2,1,0:T(1,128)} %copy.295), calls=%async_computation | async-start | bytes 8192 | tf_op jit(solution)/shard_map/all_to_all | solution.py:220
  18.6 93.7 %all-gather.2.cloned.1.call-start = ((), (), s32[]{:S(2)}) async-start(), calls=%async_computation.4 | async-start | bytes 1310720 | tf_op jit(solution)/shard_map/all_gather | solution.py:90
  22.3 79.5 %copy-start.3 = (bf16[512,256]{1,0:T(8,128)(2,1)S(1)}, bf16[512,256]{1,0:T(8,128)(2,1)}, u32[]{:S(2)}) copy-start(bf16[512,256]{1,0:T(8,128)(2,1)} %param.35) | copy-start | bytes 786436
  101.2 0.6 copy-start.28
  102.4 2.6 %copy-start.29 = (s32[8]{0:T(128)S(1)}, s32[8]{0:T(128)}, u32[]{:S(2)}) copy-start(s32[8]{0:T(128)} %copy-done.28) | copy-start | bytes 100
  107.9 46.9 %all-to-all-start.1 = ((bf16[8,256,256]{2,1,0:T(8,128)(2,1)}), bf16[8,256,256]{2,1,0:T(8,128)(2,1)}, u32[]{:S(2)}, u32[]{:S(2)}) async-start(bf16[8,256,256]{2,1,0:T(8,128)(2,1)} %get-tuple-element.34), calls=%async_computation.1 | async-start | bytes 2097152 | tf_op jit(solution)/shard_map/all_to_all | solution.py:228
  112.3 3.3 %copy-start.27 = (f32[128]{0:T(128)S(1)}, f32[128]{0:T(128)}, u32[]{:S(2)}) copy-start(f32[128]{0:T(128)} %convert_element_type.86) | copy-start | bytes 1540
  115.0 1.0 copy-start.8
  115.9 3.1 %copy-start.5 = (bf16[256,2048]{1,0:T(8,128)(2,1)S(1)}, bf16[256,2048]{1,0:T(8,128)(2,1)}, u32[]{:S(2)}) copy-start(bf16[256,2048]{1,0:T(8,128)(2,1)} %all-gather.2.cloned.1.call-done) | copy-start | bytes 3145732
  115.9 3.1 %copy-start.13 = (bf16[2048,256]{1,0:T(8,128)(2,1)S(1)}, bf16[2048,256]{1,0:T(8,128)(2,1)}, u32[]{:S(2)}) copy-start(bf16[2048,256]{1,0:T(8,128)(2,1)} %param.28) | copy-start | bytes 3145732
  119.4 6.8 %copy-start.1 = (bf16[256,256]{1,0:T(8,128)(2,1)}, bf16[256,256]{1,0:T(8,128)(2,1)S(1)}, u32[]{:S(2)}) copy-start(bf16[256,256]{1,0:T(8,128)(2,1)S(1)} %convolution_convert_fusion.1) | copy-start | bytes 393220
  122.0 5.5 %copy-start.30 = (f32[128]{0:T(128)S(1)}, f32[128]{0:T(128)}, u32[]{:S(2)}) copy-start(f32[128]{0:T(128)} %convert_element_type.82) | copy-start | bytes 1540
  126.2 4.7 %copy-start.12 = (bf16[256,4,128]{2,1,0:T(4,128)(2,1)S(1)}, bf16[256,4,128]{2,1,0:T(4,128)(2,1)}, u32[]{:S(2)}) copy-start(bf16[256,4,128]{2,1,0:T(4,128)(2,1)} %pad_maximum_fusion) | copy-start | bytes 786436
  130.9 2.0 copy-start.26
  135.9 2.0 copy-start.25
  137.9 2.2 copy-start.11
  137.9 2.2 copy-start.23
  137.9 2.3 %copy-start.21 = (pred[8,64]{1,0:T(8,128)(4,1)S(1)}, pred[8,64]{1,0:T(8,128)(4,1)}, u32[]{:S(2)}) copy-start(pred[8,64]{1,0:T(8,128)(4,1)} %iota_compare_fusion.5) | copy-start | bytes 1540
  140.0 2.8 %copy-start.15 = (bf16[8,64,2,2,128]{4,3,2,1,0:T(2,128)(2,1)}, bf16[8,64,2,2,128]{4,3,2,1,0:T(2,128)(2,1)S(1)}, u32[]{:S(2)}) copy-start(bf16[8,64,2,2,128]{4,3,2,1,0:T(2,128)(2,1)S(1)} %reshape.512) | copy-start | bytes 1572868
  140.0 2.8 %copy-start.14 = (pred[8,64,64]{1,2,0:T(8,128)(4,1)S(1)}, pred[8,64,64]{1,2,0:T(8,128)(4,1)}, u32[]{:S(2)}) copy-start(pred[8,64,64]{1,2,0:T(8,128)(4,1)} %broadcast_and_fusion) | copy-start | bytes 98308
  145.6 1.3 copy-start.4
  145.6 1.3 copy-start.9
  145.6 1.4 copy-start.22
  154.8 23.4 %all-to-all-start.2 = ((bf16[8,256,256]{2,1,0:T(8,128)(2,1)}), bf16[8,256,256]{2,1,0:T(8,128)(2,1)}, u32[]{:S(2)}, u32[]{:S(2)}) async-start(bf16[8,256,256]{2,1,0:T(8,128)(2,1)} %get-tuple-element.33), calls=%async_computation.2 | async-start | bytes 2097152 | tf_op jit(solution)/shard_map/all_to_all | solution.py:229
  160.5 7.6 %copy-start.10 = (bf16[256,4,64]{2,0,1:T(8,128)(2,1)S(1)}, bf16[256,4,64]{2,0,1:T(8,128)(2,1)}, u32[]{:S(2)}) copy-start(bf16[256,4,64]{2,0,1:T(8,128)(2,1)} %copy.291) | copy-start | bytes 393220
  160.5 58.1 %reduce-scatter.2.cloned.1.call-start = ((), (), s32[]{:S(2)}) async-start(), calls=%async_computation.5 | async-start | bytes 1310720 | tf_op jit(solution)/shard_map/reduce_scatter | solution.py:250
  162.6 5.5 %copy-start.6 = (bf16[1024,256]{0,1:T(8,128)(2,1)S(1)}, bf16[1024,256]{0,1:T(8,128)(2,1)}, u32[]{:S(2)}) copy-start(bf16[1024,256]{0,1:T(8,128)(2,1)} %all_gather.10) | copy-start | bytes 1572868
  168.1 1.8 copy-start.20
  169.9 1.9 copy-start.2
  172.7 1.5 copy-start.19
  172.8 1.5 copy-start.31
  175.9 1.3 copy-start.7
  182.9 1.9 copy-start.18
  184.8 2.3 %copy-start.24 = (pred[256]{0:T(512)(128)(4,1)S(1)}, pred[256]{0:T(512)(128)(4,1)}, u32[]{:S(2)}) copy-start(pred[256]{0:T(512)(128)(4,1)} %get-tuple-element.28) | copy-start | bytes 772
Sparse Core Ops, SparseCore 0:
  22.4 18.0 all-gather.1
  192.5 26.0 reduce-scatter.1
where the time goes:
time: 227 us; the launch traced here: 225 us
  blocking collectives  61.1 us (27%)
  local copies, waits for them, and re-layouts  50.7 us (22%)
  other arithmetic  32.1 us (14%)
  waiting for transfers between devices  25.6 us (11%)
  matrix products  23.6 us (10%)
  starting transfers between devices  17.7 us (8%)
  between operations  14.8 us (7%)
    all_gather x1, blocking collectives, body(): lax.all_gather(prefix_root_values, 'dp', axis=0, tiled=True)  31.3 us
    all_gather x1, blocking collectives, body(): lax.all_gather(prefix_root_keys, 'dp', axis=0, tiled=True)  29.8 us
    reduce_scatter x1, waiting for transfers between devices, body(): lax.psum_scatter(jnp.dot(attn, w_out, preferred_element_type=jnp.float32)...  25.5 us
    all_to_all x1, starting transfers between devices, body(): lax.all_to_all(block_slot[:, None], 'dp', split_axis=0, concat_axis=0, ti...  7.28 us
    all_to_all x1, starting transfers between devices, body(): lax.all_to_all(sent_values, 'dp', split_axis=0, concat_axis=0, tiled=True)  5.7 us
    unnamed x67, local copies, waits for them, and re-layouts  5.58 us
    gather x2, local copies, waits for them, and re-layouts, body(): jnp.take(req_summed.reshape(requests * capacity, kv_heads, query_group, h...  5.41 us
  transfers between devices with their start and end apart: 5, of which 1 were waited for; matrix products, arithmetic and copies ran while one was open for 37% of the time, Pallas kernels for 0%

commit v1 on v0

--- a/solution.py
+++ b/solution.py
@@ -9,6 +9,20 @@
 EPS = 1e-06
 THETA = 1000000.0
 MASKED = -1e30
+
+
+def lift_the_threads(block_here, array_axis, in_array):
+    o_now = block_here.shape
+    val2 = block_here.reshape(
+        *o_now[:array_axis], in_array, o_now[array_axis] // in_array, *o_now[array_axis + 1 :]
+    )
+    return jnp.moveaxis(val2, array_axis, 0)
+
+
+def find_values(inner_x, join_dim):
+    small = list(inner_x.shape[1:])
+    small[join_dim] *= inner_x.shape[0]
+    return jnp.moveaxis(inner_x, 0, join_dim).reshape(small)
 
 
 def rms_rows(values, gain):
@@ -224,8 +238,21 @@
     own_values = mid_values.reshape(MID_DEV, MID_LEN, key_width)
     sent_keys = jnp.take(own_keys, wanted, axis=0)
     sent_values = jnp.take(own_values, wanted, axis=0)
+
+    def measure_squares(load, chip_axis, my_data, state=0):
+        tmp, r2 = (lax.axis_size(chip_axis), lax.axis_index(chip_axis))
+        local_part = lift_the_threads(load, my_data, tmp)
+        samples = [local_part[r2]]
+        for ii in range(1, tmp):
+            q_next = local_part[r2 ^ ii]
+            samples.append(
+                lax.ppermute(q_next, axis_name=chip_axis, perm=[(jj, jj ^ ii) for jj in range(tmp)])
+            )
+        local_part = jnp.stack(samples)[r2 ^ jnp.arange(tmp)]
+        return find_values(local_part, state)
+
     got_keys, got_values = (
-        lax.all_to_all(sent_keys, "dp", split_axis=0, concat_axis=0, tiled=True),
+        measure_squares(sent_keys, "dp", 0),
         lax.all_to_all(sent_values, "dp", split_axis=0, concat_axis=0, tiled=True),
     )
     middle_output, middle_log_sum = attend_over_block(

time: 227 us -> 252 us (1.11)
  waiting for transfers between devices: 25.6 us -> 46 us
  starting transfers between devices: 17.7 us -> 24.9 us
    ppermute x0 -> x7, waiting for transfers between devices: none -> 23 us  [measure_squares(): lax.ppermute(q_next, axis_name=chip_axis, perm=[(jj, jj ^ ii) for jj in r...]
    ppermute x0 -> x7, starting transfers between devices: none -> 13.1 us  [measure_squares(): lax.ppermute(q_next, axis_name=chip_axis, perm=[(jj, jj ^ ii) for jj in r...]
    all_to_all x1 -> x0, starting transfers between devices: 4.42 us -> none  [body(): lax.all_to_all(sent_keys, 'dp', split_axis=0, concat_axis=0, tiled=True)]
    gather x0 -> x2, local copies, waits for them, and re-layouts: none -> 3.13 us  [measure_squares(): local_part = jnp.stack(samples)[r2 ^ jnp.arange(tmp)]]
    reduce_scatter x1, waiting for transfers between devices: 25.5 us -> 23 us  [body(): lax.psum_scatter(jnp.dot(attn, w_out, preferred_element_type=jnp.float32)...]
    unnamed x67 -> x96, local copies, waits for them, and re-layouts: 5.58 us -> 5.73 us
  transfers between devices with their start and end apart: 5 -> 11, of which waited for: 1 -> 5; matrix products, arithmetic and copies ran while one was open for 37% -> 34% of each run, Pallas kernels for 0% -> 0%
where the time goes in v1:
time: 252 us; the launch traced here: 251 us
  blocking collectives  61.1 us (24%)
  local copies, waits for them, and re-layouts  51.2 us (20%)
  waiting for transfers between devices  46 us (18%)
  other arithmetic  32 us (13%)
  starting transfers between devices  24.9 us (10%)
  matrix products  21.2 us (8%)
  between operations  15 us (6%)
    all_gather x1, blocking collectives, body(): lax.all_gather(prefix_root_values, 'dp', axis=0, tiled=True)  31.3 us
    all_gather x1, blocking collectives, body(): lax.all_gather(prefix_root_keys, 'dp', axis=0, tiled=True)  29.8 us
    reduce_scatter x1, waiting for transfers between devices, body(): lax.psum_scatter(jnp.dot(attn, w_out, preferred_element_type=jnp.float32)...  23 us
    ppermute x7, waiting for transfers between devices, measure_squares(): lax.ppermute(q_next, axis_name=chip_axis, perm=[(jj, jj ^ ii) for jj in r...  23 us
    ppermute x7, starting transfers between devices, measure_squares(): lax.ppermute(q_next, axis_name=chip_axis, perm=[(jj, jj ^ ii) for jj in r...  13.1 us
    all_to_all x1, starting transfers between devices, body(): lax.all_to_all(block_slot[:, None], 'dp', split_axis=0, concat_axis=0, ti...  7.28 us
    unnamed x96, local copies, waits for them, and re-layouts  5.73 us
  transfers between devices with their start and end apart: 11, of which 5 were waited for; matrix products, arithmetic and copies ran while one was open for 34% of the time, Pallas kernels for 0%

profile of v1, /device:TPU:0, one launch (start us, length us, event | category | flops | bytes accessed | tf_op | source)
XLA Modules:
  0.0 251.3 jit_solution(1909418435959537481)
XLA Ops:
  7.2 0.9 convert_reduce_fusion
  9.0 0.9 select_reduce_fusion.8
  10.7 7.3 %all-to-all-start = ((s32[8,1,1]{2,1,0:T(1,128)}), s32[8,1,1]{2,1,0:T(1,128)S(1)}, u32[]{:S(2)}, u32[]{:S(2)}) async-start(s32[8,1,1]{2,1,0:T(1,128)} %copy.325), calls=%async_computation | async-start | bytes 8192 | tf_op jit(solution)/shard_map/all_to_all | solution.py:234
  18.0 1.1 fusion.44
  19.8 1.8 fusion.46
  22.9 1.3 iota_compare_fusion.5
  26.5 1.2 convert_element_type.86
  27.7 1.1 convert_element_type.82
  29.5 1.0 copy.323
  30.5 1.7 reshape.542
  33.0 29.8 %all_gather.10 = bf16[1024,256]{0,1:T(8,128)(2,1)} all-gather(bf16[128,256]{0,1:T(8,128)(2,1)S(1)} %copy.323), channel_id=1, replica_groups=mesh['dp'=8,'head'=4] {'dp'}, dimensions={0}, use_global_device_ids=true | all-gather | bytes 589824 | tf_op jit(solution)/shard_map/all_gather | solution.py:202
  62.7 31.3 %all_gather.11 = bf16[1024,256]{1,0:T(8,128)(2,1)S(1)} all-gather(bf16[128,256]{1,0:T(8,128)(2,1)S(1)} %copy-done.25), channel_id=1, replica_groups=mesh['dp'=8,'head'=4] {'dp'}, dimensions={0}, use_global_device_ids=true | all-gather | bytes 589824 | tf_op jit(solution)/shard_map/all_gather | solution.py:203
  94.1 1.1 copy.347
  99.2 1.6 gather_fusion.10
  100.9 1.6 gather_fusion.8
  102.5 2.8 %broadcast_select_fusion = (bf16[8,256,256]{2,1,0:T(8,128)(2,1)}, bf16[8,256,256]{2,1,0:T(8,128)(2,1)S(1)}) fusion(bf16[8,256,256]{2,1,0:T(8,128)(2,1)} %gather_fusion.10, pred[8]{0:T(512)(128)(4,1)S(1)} %compare_and_fusion.2, bf16[8,256,256]{2,1,0:T(8,128)(2,1)} %gather_fusion.8), kind=kLoop, calls=%fused_computation.49 | loop fusion | flops 1048576 | bytes 4194312 | tf_op jit(solution)/shard_map/jit(_take)/select_n | solution.py:240
  105.3 4.2 %all-to-all-start.1 = ((bf16[8,256,256]{2,1,0:T(8,128)(2,1)}), bf16[8,256,256]{2,1,0:T(8,128)(2,1)}, u32[]{:S(2)}, u32[]{:S(2)}) async-start(bf16[8,256,256]{2,1,0:T(8,128)(2,1)} %get-tuple-element.40), calls=%async_computation.1 | async-start | bytes 2097152 | tf_op jit(solution)/shard_map/all_to_all | solution.py:256
  109.9 4.5 %collective-permute-start.6 = (bf16[1,256,256]{2,1,0:T(8,128)(2,1)S(1)}, bf16[1,256,256]{2,1,0:T(8,128)(2,1)S(1)}, u32[]{:S(2)}, u32[]{:S(2)}) collective-permute-start(bf16[1,256,256]{2,1,0:T(8,128)(2,1)S(1)} %get-tuple-element.22), channel_id=1, source_target_pairs={{0,28},{4,24},{8,20},{12,16},{16,12},{20,8},{24,4},{28,0},{1,29},{... | collective-permute-start | bytes 393224 | tf_op jit(solution)/shard_map/ppermute | solution.py:249
  115.4 2.2 collective-permute-start.3
  117.6 1.6 collective-permute-start
  119.2 1.2 multiply_cosine_fusion
  120.5 2.7 %collective-permute-done = bf16[1,256,256]{2,1,0:T(8,128)(2,1)S(1)} collective-permute-done((bf16[1,256,256]{2,1,0:T(8,128)(2,1)S(1)}, bf16[1,256,256]{2,1,0:T(8,128)(2,1)S(1)}, u32[]{:S(2)}, u32[]{:S(2)}) %collective-permute-start) | collective-permute-done | bytes 131104 | tf_op jit(solution)/shard_map/ppermute | solution.py:249
  123.7 7.9 %collective-permute-done.1 = bf16[1,256,256]{2,1,0:T(8,128)(2,1)S(1)} collective-permute-done((bf16[1,256,256]{2,1,0:T(8,128)(2,1)S(1)}, bf16[1,256,256]{2,1,0:T(8,128)(2,1)S(1)}, u32[]{:S(2)}, u32[]{:S(2)}) %collective-permute-start.1) | collective-permute-done | bytes 131104 | tf_op jit(solution)/shard_map/ppermute | solution.py:249
  131.6 3.3 %collective-permute-start.2 = (bf16[1,256,256]{2,1,0:T(8,128)(2,1)S(1)}, bf16[1,256,256]{2,1,0:T(8,128)(2,1)S(1)}, u32[]{:S(2)}, u32[]{:S(2)}) collective-permute-start(bf16[1,256,256]{2,1,0:T(8,128)(2,1)S(1)} %get-tuple-element.26), channel_id=1, source_target_pairs={{0,12},{4,8},{8,4},{12,0},{16,28},{20,24},{24,20},{28,16},{1,13},{... | collective-permute-start | bytes 393224 | tf_op jit(solution)/shard_map/ppermute | solution.py:249
  134.9 3.1 %collective-permute-done.2 = bf16[1,256,256]{2,1,0:T(8,128)(2,1)S(1)} collective-permute-done((bf16[1,256,256]{2,1,0:T(8,128)(2,1)S(1)}, bf16[1,256,256]{2,1,0:T(8,128)(2,1)S(1)}, u32[]{:S(2)}, u32[]{:S(2)}) %collective-permute-start.2) | collective-permute-done | bytes 131104 | tf_op jit(solution)/shard_map/ppermute | solution.py:249
  138.0 9.2 %collective-permute-done.3 = bf16[1,256,256]{2,1,0:T(8,128)(2,1)S(1)} collective-permute-done((bf16[1,256,256]{2,1,0:T(8,128)(2,1)S(1)}, bf16[1,256,256]{2,1,0:T(8,128)(2,1)S(1)}, u32[]{:S(2)}, u32[]{:S(2)}) %collective-permute-start.3) | collective-permute-done | bytes 131104 | tf_op jit(solution)/shard_map/ppermute | solution.py:249
  147.3 1.0 copy-done.9
  148.3 1.8 gather_fusion.1
  150.1 1.3 copy.332
  151.4 2.6 %fusion.90 = f32[256,512]{1,0:T(8,128)S(1)} fusion(bf16[256,2048]{1,0:T(8,128)(2,1)} %all-gather.2.cloned.1.call-done, bf16[2048,512]{1,0:T(8,128)(2,1)} %param.26), kind=kOutput, calls=%fused_computation.207 | convolution fusion | flops 536870912 | bytes 3670016 | tf_op jit(solution)/shard_map/dot_general | solution.py:107
  156.3 1.1 pad_maximum_fusion
  158.5 2.6 %gather_fusion.3 = bf16[512,256]{1,0:T(8,128)(2,1)} fusion(bf16[256,256]{1,0:T(8,128)(2,1)S(1)} %convolution_convert_fusion.1, s32[1024]{0:T(1024)S(1)} %pad_clamp_fusion.7), kind=kCustom, calls=%fused_computation.9 | custom fusion | bytes 526336 | tf_op jit(solution)/shard_map/jit(_take)/gather | solution.py:153
  161.1 1.7 gather.46
  162.8 2.5 multiply_reduce_fusion.1
  165.3 1.1 copy.310
  167.8 2.1 gather_fusion
  170.0 2.0 gather_fusion.9
  172.0 1.0 broadcast_select_fusion.2
  173.0 2.0 reshape.545
  175.0 2.2 gather_fusion.6
  177.2 1.0 broadcast_select_fusion.3
  178.2 1.2 reshape.541
  179.6 2.6 %fusion.89 = (f32[8,64,2,2]{1,3,2,0:T(2,128)S(1)}, f32[8,64,2,2,64]{1,4,3,2,0:T(8,128)}) fusion(bf16[8,64,2,128,1]{3,2,1,0,4:T(2,128)(2,1)} %bitcast.193, bf16[8,64,2,2,128]{4,3,2,1,0:T(2,128)(2,1)S(1)} %reshape.541, pred[8,64]{1,0:T(8,128)(4,1)S(1)} %copy-done.33), kind=kOutput, calls=%fused_computation.206 | convolution fusion | flops 33945600 | bytes 1319424 | tf_op jit(solution)/shard_map/rskgd,rlkd->rskgl/dot_general | solution.py:166
  182.2 1.7 fusion.88
  183.9 1.1 copy.368
  185.0 2.5 fusion.42
  189.4 2.2 gather_fusion.4
  191.6 2.2 copy.346
  194.0 1.0 gather_fusion.11
  195.7 1.0 gather_fusion.7
  197.4 2.0 bitcast_reduce_fusion.1
  199.5 1.3 copy-done.8
  200.8 0.9 fusion.9
  203.8 1.5 gather_fusion.2
  205.3 1.0 copy.338
  206.4 0.8 bitcast_reduce_fusion
  207.3 0.9 fusion.1
  208.2 1.0 copy-done.2
  209.2 1.7 copy.348
  211.0 2.3 fusion.16
  214.1 1.3 gather_fusion.5
  215.5 3.5 %fusion.37 = bf16[256,2,2,128]{0,3,2,1:T(8,128)(2,1)S(1)} fusion(bf16[1024,2,128,1]{0,2,3,1:T(8,128)(2,1)} %bitcast.192, f32[2,256,2,1024]{3,1,2,0:T(8,128)} %copy-done.2, f32[256,2,2]{0,2,1:T(2,128)S(1)} %fusion.74, f32[256,2,2,128]{0,3,2,1:T(8,128)} %copy.346, f32[256,2,2]{0,2,1:T(2,128)S(1)} %get-tuple-element.16, ...), kind=kOutput, calls=%fused_computation.53 | convolution fusion | flops 272891904 | bytes 5788160 | tf_op jit(solution)/shard_map/tkgs,skd->tkgd/dot_general | solution.py:217
  219.1 1.7 convolution_convert_fusion
  221.5 23.0 %reduce-scatter.2.cloned.1.call-done = bf16[64,2048]{1,0:T(8,128)(2,1)} async-done(((bf16[256,2048]{1,0:T(8,128)(2,1)}), bf16[64,2048]{1,0:T(8,128)(2,1)}) %reduce-scatter.2.cloned.1.call-update) | async-done | bytes 262160 | tf_op jit(solution)/shard_map/reduce_scatter | solution.py:277
  (180 shorter events, 25.7 us)
Async XLA Ops:
  7.2 211.9 %copy-start = (bf16[512,2048]{1,0:T(8,128)(2,1)S(1)}, bf16[512,2048]{1,0:T(8,128)(2,1)}, u32[]{:S(2)}) copy-start(bf16[512,2048]{1,0:T(8,128)(2,1)} %param.31) | copy-start | bytes 6291460
  7.2 25.0 %copy-start.20 = (bf16[512,256]{1,0:T(8,128)(2,1)S(1)}, bf16[512,256]{1,0:T(8,128)(2,1)}, u32[]{:S(2)}) copy-start(bf16[512,256]{1,0:T(8,128)(2,1)} %param.38) | copy-start | bytes 786436
  7.2 55.6 %copy-start.25 = (bf16[128,256]{1,0:T(8,128)(2,1)S(1)}, bf16[128,256]{1,0:T(8,128)(2,1)}, u32[]{:S(2)}) copy-start(bf16[128,256]{1,0:T(8,128)(2,1)} %param.33) | copy-start | bytes 196612
  10.7 85.2 %all-to-all-start = ((s32[8,1,1]{2,1,0:T(1,128)}), s32[8,1,1]{2,1,0:T(1,128)S(1)}, u32[]{:S(2)}, u32[]{:S(2)}) async-start(s32[8,1,1]{2,1,0:T(1,128)} %copy.325), calls=%async_computation | async-start | bytes 8192 | tf_op jit(solution)/shard_map/all_to_all | solution.py:234
  18.0 133.5 %all-gather.2.cloned.1.call-start = ((), (), s32[]{:S(2)}) async-start(), calls=%async_computation.3 | async-start | bytes 1310720 | tf_op jit(solution)/shard_map/all_gather | solution.py:104
  21.6 74.5 %copy-start.41 = (s32[1,8]{1,0:T(1,128)S(1)}, s32[1,8]{1,0:T(1,128)}, u32[]{:S(2)}) copy-start(s32[1,8]{1,0:T(1,128)} %param.41) | copy-start | bytes 100
  21.6 74.6 %copy-start.39 = (s32[1,256]{1,0:T(1,128)S(1)}, s32[1,256]{1,0:T(1,128)}, u32[]{:S(2)}) copy-start(s32[1,256]{1,0:T(1,128)} %param.40) | copy-start | bytes 3076
  21.6 77.6 %copy-start.3 = (bf16[512,256]{1,0:T(8,128)(2,1)S(1)}, bf16[512,256]{1,0:T(8,128)(2,1)}, u32[]{:S(2)}) copy-start(bf16[512,256]{1,0:T(8,128)(2,1)} %param.35) | copy-start | bytes 786436
  62.7 38.1 %copy-start.4 = (bf16[512,256]{1,0:T(8,128)(2,1)S(1)}, bf16[512,256]{1,0:T(8,128)(2,1)}, u32[]{:S(2)}) copy-start(bf16[512,256]{1,0:T(8,128)(2,1)} %param.34) | copy-start | bytes 786436
  105.3 103.9 %all-to-all-start.1 = ((bf16[8,256,256]{2,1,0:T(8,128)(2,1)}), bf16[8,256,256]{2,1,0:T(8,128)(2,1)}, u32[]{:S(2)}, u32[]{:S(2)}) async-start(bf16[8,256,256]{2,1,0:T(8,128)(2,1)} %get-tuple-element.40), calls=%async_computation.1 | async-start | bytes 2097152 | tf_op jit(solution)/shard_map/all_to_all | solution.py:256
  109.5 134.9 %reduce-scatter.2.cloned.1.call-start = ((), (), s32[]{:S(2)}) async-start(), calls=%async_computation.4 | async-start | bytes 1310720 | tf_op jit(solution)/shard_map/reduce_scatter | solution.py:277
  109.9 37.4 %collective-permute-start.6 = (bf16[1,256,256]{2,1,0:T(8,128)(2,1)S(1)}, bf16[1,256,256]{2,1,0:T(8,128)(2,1)S(1)}, u32[]{:S(2)}, u32[]{:S(2)}) collective-permute-start(bf16[1,256,256]{2,1,0:T(8,128)(2,1)S(1)} %get-tuple-element.22), channel_id=1, source_target_pairs={{0,28},{4,24},{8,20},{12,16},{16,12},{20,8},{24,4},{28,0},{1,29},{... | collective-permute-start | bytes 393224 | tf_op jit(solution)/shard_map/ppermute | solution.py:249
  114.3 33.0 %collective-permute-start.5 = (bf16[1,256,256]{2,1,0:T(8,128)(2,1)S(1)}, bf16[1,256,256]{2,1,0:T(8,128)(2,1)S(1)}, u32[]{:S(2)}, u32[]{:S(2)}) collective-permute-start(bf16[1,256,256]{2,1,0:T(8,128)(2,1)S(1)} %get-tuple-element.23), channel_id=1, source_target_pairs={{0,24},{4,28},{8,16},{12,20},{16,8},{20,12},{24,0},{28,4},{1,25},{... | collective-permute-start | bytes 393224 | tf_op jit(solution)/shard_map/ppermute | solution.py:249
  114.8 32.4 %collective-permute-start.4 = (bf16[1,256,256]{2,1,0:T(8,128)(2,1)S(1)}, bf16[1,256,256]{2,1,0:T(8,128)(2,1)S(1)}, u32[]{:S(2)}, u32[]{:S(2)}) collective-permute-start(bf16[1,256,256]{2,1,0:T(8,128)(2,1)S(1)} %get-tuple-element.24), channel_id=1, source_target_pairs={{0,20},{4,16},{8,28},{12,24},{16,4},{20,0},{24,12},{28,8},{1,21},{... | collective-permute-start | bytes 393224 | tf_op jit(solution)/shard_map/ppermute | solution.py:249
  115.4 31.8 %collective-permute-start.3 = (bf16[1,256,256]{2,1,0:T(8,128)(2,1)S(1)}, bf16[1,256,256]{2,1,0:T(8,128)(2,1)S(1)}, u32[]{:S(2)}, u32[]{:S(2)}) collective-permute-start(bf16[1,256,256]{2,1,0:T(8,128)(2,1)S(1)} %get-tuple-element.25), channel_id=1, source_target_pairs={{0,16},{4,20},{8,24},{12,28},{16,0},{20,4},{24,8},{28,12},{1,17},{... | collective-permute-start | bytes 393224 | tf_op jit(solution)/shard_map/ppermute | solution.py:249
  117.6 5.6 %collective-permute-start = (bf16[1,256,256]{2,1,0:T(8,128)(2,1)S(1)}, bf16[1,256,256]{2,1,0:T(8,128)(2,1)S(1)}, u32[]{:S(2)}, u32[]{:S(2)}) collective-permute-start(bf16[1,256,256]{2,1,0:T(8,128)(2,1)S(1)} %get-tuple-element.28), channel_id=1, source_target_pairs={{0,4},{4,0},{8,12},{12,8},{16,20},{20,16},{24,28},{28,24},{1,5},{5... | collective-permute-start | bytes 393224 | tf_op jit(solution)/shard_map/ppermute | solution.py:249
  123.2 8.5 %collective-permute-start.1 = (bf16[1,256,256]{2,1,0:T(8,128)(2,1)S(1)}, bf16[1,256,256]{2,1,0:T(8,128)(2,1)S(1)}, u32[]{:S(2)}, u32[]{:S(2)}) collective-permute-start(bf16[1,256,256]{2,1,0:T(8,128)(2,1)S(1)} %get-tuple-element.27), channel_id=1, source_target_pairs={{0,8},{4,12},{8,0},{12,4},{16,24},{20,28},{24,16},{28,20},{1,9},{5... | collective-permute-start | bytes 393224 | tf_op jit(solution)/shard_map/ppermute | solution.py:249
  131.6 6.4 %collective-permute-start.2 = (bf16[1,256,256]{2,1,0:T(8,128)(2,1)S(1)}, bf16[1,256,256]{2,1,0:T(8,128)(2,1)S(1)}, u32[]{:S(2)}, u32[]{:S(2)}) collective-permute-start(bf16[1,256,256]{2,1,0:T(8,128)(2,1)S(1)} %get-tuple-element.26), channel_id=1, source_target_pairs={{0,12},{4,8},{8,4},{12,0},{16,28},{20,24},{24,20},{28,16},{1,13},{... | collective-permute-start | bytes 393224 | tf_op jit(solution)/shard_map/ppermute | solution.py:249
  147.3 1.0 copy-start.9
  151.4 3.2 %copy-start.40 = (f32[128]{0:T(128)S(1)}, f32[128]{0:T(128)}, u32[]{:S(2)}) copy-start(f32[128]{0:T(128)} %convert_element_type.86) | copy-start | bytes 1540
  155.0 3.1 %copy-start.6 = (bf16[256,2048]{1,0:T(8,128)(2,1)S(1)}, bf16[256,2048]{1,0:T(8,128)(2,1)}, u32[]{:S(2)}) copy-start(bf16[256,2048]{1,0:T(8,128)(2,1)} %all-gather.2.cloned.1.call-done) | copy-start | bytes 3145732
  155.0 3.1 %copy-start.16 = (bf16[2048,256]{1,0:T(8,128)(2,1)S(1)}, bf16[2048,256]{1,0:T(8,128)(2,1)}, u32[]{:S(2)}) copy-start(bf16[2048,256]{1,0:T(8,128)(2,1)} %param.28) | copy-start | bytes 3145732
  158.5 6.8 %copy-start.1 = (bf16[256,256]{1,0:T(8,128)(2,1)}, bf16[256,256]{1,0:T(8,128)(2,1)S(1)}, u32[]{:S(2)}) copy-start(bf16[256,256]{1,0:T(8,128)(2,1)S(1)} %convolution_convert_fusion.1) | copy-start | bytes 393220
  161.1 5.5 %copy-start.42 = (f32[128]{0:T(128)S(1)}, f32[128]{0:T(128)}, u32[]{:S(2)}) copy-start(f32[128]{0:T(128)} %convert_element_type.82) | copy-start | bytes 1540
  165.3 4.7 %copy-start.15 = (bf16[256,4,128]{2,1,0:T(4,128)(2,1)S(1)}, bf16[256,4,128]{2,1,0:T(4,128)(2,1)}, u32[]{:S(2)}) copy-start(bf16[256,4,128]{2,1,0:T(4,128)(2,1)} %pad_maximum_fusion) | copy-start | bytes 786436
  170.0 2.0 copy-start.38
  175.0 2.2 copy-start.37
  177.2 2.2 copy-start.14
  177.2 2.2 copy-start.35
  177.2 2.4 copy-start.33
  179.4 2.8 %copy-start.19 = (bf16[8,64,2,2,128]{4,3,2,1,0:T(2,128)(2,1)}, bf16[8,64,2,2,128]{4,3,2,1,0:T(2,128)(2,1)S(1)}, u32[]{:S(2)}) copy-start(bf16[8,64,2,2,128]{4,3,2,1,0:T(2,128)(2,1)S(1)} %reshape.541) | copy-start | bytes 1572868
  179.4 2.8 %copy-start.17 = (pred[8,64,64]{1,2,0:T(8,128)(4,1)S(1)}, pred[8,64,64]{1,2,0:T(8,128)(4,1)}, u32[]{:S(2)}) copy-start(pred[8,64,64]{1,2,0:T(8,128)(4,1)} %broadcast_and_fusion) | copy-start | bytes 98308
  185.0 2.5 copy-start.18
  185.0 2.9 %copy-start.5 = (f32[8,64,2,2,64]{1,4,3,2,0:T(8,128)S(1)}, f32[8,64,2,2,64]{1,4,3,2,0:T(8,128)}, u32[]{:S(2)}) copy-start(f32[8,64,2,2,64]{1,4,3,2,0:T(8,128)} %get-tuple-element.53) | copy-start | bytes 1572868
  185.0 2.9 %copy-start.11 = (bf16[8,64,2,128]{3,2,1,0:T(2,128)(2,1)S(1)}, bf16[8,64,2,128]{3,2,1,0:T(2,128)(2,1)}, u32[]{:S(2)}) copy-start(bf16[8,64,2,128]{3,2,1,0:T(2,128)(2,1)} %reshape.546) | copy-start | bytes 786436
  185.0 2.9 %copy-start.34 = (pred[8,64]{1,0:T(8,128)(4,1)S(1)}, pred[8,64]{1,0:T(8,128)(4,1)}, u32[]{:S(2)}) copy-start(pred[8,64]{1,0:T(8,128)(4,1)} %iota_compare_fusion.5) | copy-start | bytes 1540
  188.5 5.2 %copy-start.23 = (f32[8,64,2,2]{1,3,2,0:T(2,128)S(1)}, f32[8,64,2,2]{1,3,2,0:T(2,128)}, u32[]{:S(2)}) copy-start(f32[8,64,2,2]{1,3,2,0:T(2,128)} %get-tuple-element.6) | copy-start | bytes 24580
  188.5 5.2 %copy-start.24 = (f32[8,64,2,2]{1,3,2,0:T(2,128)S(1)}, f32[8,64,2,2]{1,3,2,0:T(2,128)}, u32[]{:S(2)}) copy-start(f32[8,64,2,2]{1,3,2,0:T(2,128)} %get-tuple-element.7) | copy-start | bytes 24580
  188.5 5.5 %copy-start.28 = (s32[1024]{0:T(1024)S(1)}, s32[1024]{0:T(1024)}, u32[]{:S(2)}) copy-start(s32[1024]{0:T(1024)} %pad_clamp_fusion.5) | copy-start | bytes 12292
  191.6 4.2 %copy-start.10 = (f32[8,64,2,2]{3,2,1,0:T(2,128)S(1)}, f32[8,64,2,2]{3,2,1,0:T(2,128)}, u32[]{:S(2)}) copy-start(f32[8,64,2,2]{3,2,1,0:T(2,128)} %copy.368) | copy-start | bytes 24580
  196.7 4.1 %copy-start.29 = (pred[8,256]{1,0:T(8,128)(4,1)S(1)}, pred[8,256]{1,0:T(8,128)(4,1)}, u32[]{:S(2)}) copy-start(pred[8,256]{1,0:T(8,128)(4,1)} %iota_compare_fusion.1) | copy-start | bytes 6148
  199.4 1.3 copy-start.8
  199.5 6.9 %copy-start.7 = (bf16[1024,256]{0,1:T(8,128)(2,1)S(1)}, bf16[1024,256]{0,1:T(8,128)(2,1)}, u32[]{:S(2)}) copy-start(bf16[1024,256]{0,1:T(8,128)(2,1)} %all_gather.10) | copy-start | bytes 1572868
  199.5 6.9 %copy-start.12 = (bf16[256,4,64]{2,0,1:T(8,128)(2,1)S(1)}, bf16[256,4,64]{2,0,1:T(8,128)(2,1)}, u32[]{:S(2)}) copy-start(bf16[256,4,64]{2,0,1:T(8,128)(2,1)} %copy.321) | copy-start | bytes 393220
  199.5 6.9 %copy-start.13 = (bf16[256,4,64]{2,0,1:T(8,128)(2,1)S(1)}, bf16[256,4,64]{2,0,1:T(8,128)(2,1)}, u32[]{:S(2)}) copy-start(bf16[256,4,64]{2,0,1:T(8,128)(2,1)} %copy.322) | copy-start | bytes 393220
  201.7 0.6 copy-start.21
  206.3 0.9 copy-start.26
  206.4 0.9 copy-start.31
  207.2 2.0 copy-start.2
  207.2 1.9 copy-start.27
  207.3 1.9 copy-start.36
  209.2 1.8 copy-start.22
  209.2 1.8 copy-start.30
  213.9 1.6 copy-start.32
Sparse Core Ops, SparseCore 0:
  21.8 18.0 all-gather.1
  220.9 23.5 reduce-scatter.1
